TPU v7x, 128 devices: a whole 4x4x4 slice. The times are simulated.
128 devices in a mesh: blk: 8 (over x, z_lo), grp: 16 (over z_hi, y, core).
Axes of the slice: x: 4, y: 4, z: 4 (z_hi: 2, z_lo: 2; z = z_hi * 2 + z_lo), core: 2. Of those that a mesh axis runs over, the one named last changes fastest.
Arguments:
- queries: bfloat16 [65536, 4096], P(('blk', 'grp')), may hold values from -8 to 8
- passages: bfloat16 [16384, 4096], P(('blk', 'grp')), may hold values from -0.75 to 0.75
- positive_ids: int32 [65536], P(('blk', 'grp')), may hold values from 0 to 1023
- hard_ids: int32 [65536, 1], P(('blk', 'grp')), may hold values from 0 to 2047, as said below
Outputs:
- loss: float32 [], replicated
- loss_slope_by_question: bfloat16 [65536, 4096], P(('blk', 'grp'))
- grad_passages: bfloat16 [16384, 4096], P(('blk', 'grp'))
Inputs may be any that keep to these rules, and one draw needn't show every extreme that they name: `hard_ids`: of the 512 entries of one device, at most 64 name passages of any one grp index (rows g * 128 to g * 128 + 127 of the pool); in every batch shard one grp index receives exactly 64 from each device of the shard.
All inputs are finite; a program needn't handle non-finite values.
Results may differ from a plain program's by a relative error of at most 0.017.
Values may be sent and summed in bfloat16 or wider, within the bound.
A program may use at most 192 MiB of HBM per device.

v0:
```python
import jax
import jax.numpy as jnp
from jax import lax
from jax.sharding import PartitionSpec as P

logit_scaling_coefficient = 20.0


def shards(queries, passages, positive_ids, hard_ids):
    query_rows, embedding_width = queries.shape
    own_rows = passages.shape[0]
    group_count = lax.axis_size("grp")
    hard_count = hard_ids.shape[1]
    loop_block = lax.all_gather(passages, "blk", axis=0, tiled=True)
    flat_ids = hard_ids.reshape(-1)
    seat_total_number = flat_ids.shape[0]
    owner_index = flat_ids // own_rows
    local_row = flat_ids % own_rows
    member = (owner_index[:, None] == jnp.arange(group_count, dtype=jnp.int32)[None, :]).astype(
        jnp.int32
    )
    before = jnp.sum((jnp.cumsum(member, axis=0) - member) * member, axis=1)
    capacity = 2 * seat_total_number // group_count
    seat_index = owner_index * capacity + before
    request = jnp.zeros((group_count * capacity,), jnp.int32).at[seat_index].set(local_row + 1)
    request = request.reshape(group_count, capacity)
    asked_rows = lax.all_to_all(request, "grp", split_axis=0, concat_axis=0, tiled=True)
    picked = jnp.take(passages, jnp.maximum(asked_rows - 1, 0), axis=0)
    picked = jnp.where((asked_rows > 0)[:, :, None], picked, jnp.zeros_like(picked))
    returned = lax.all_to_all(picked, "grp", split_axis=0, concat_axis=0, tiled=True)
    hard_rows = returned.reshape(group_count * capacity, embedding_width)[seat_index]
    tough_candidate_tile = hard_rows.reshape(query_rows, hard_count, embedding_width)
    affinity_scores_raw = logit_scaling_coefficient * lax.dot_general(
        queries, loop_block, (((1,), (1,)), ((), ())), preferred_element_type=jnp.float32
    )
    difficult_distractor_scores_raw = logit_scaling_coefficient * jnp.einsum(
        "qd,qhd->qh", queries, tough_candidate_tile, preferred_element_type=jnp.float32
    )
    top_score = jnp.maximum(
        jnp.max(affinity_scores_raw, 1), jnp.max(difficult_distractor_scores_raw, 1)
    )
    total = jnp.sum(jnp.exp(affinity_scores_raw - top_score[:, None]), 1) + jnp.sum(
        jnp.exp(difficult_distractor_scores_raw - top_score[:, None]), 1
    )
    log_total = top_score + jnp.log(total)
    positive_mask = (
        positive_ids[:, None] == jnp.arange(loop_block.shape[0], dtype=jnp.int32)[None, :]
    )
    positive_logit = jnp.sum(jnp.where(positive_mask, affinity_scores_raw, 0.0), 1)
    loss_sum = lax.psum(jnp.sum(log_total - positive_logit), ("blk", "grp"))
    loss = loss_sum / (query_rows * lax.axis_size("blk") * group_count)
    minibatch_normalized_probability = (
        jnp.exp(affinity_scores_raw - log_total[:, None]) - positive_mask.astype(jnp.float32)
    ).astype(jnp.bfloat16)
    tough_candidate_likelihood = jnp.exp(
        difficult_distractor_scores_raw - log_total[:, None]
    ).astype(jnp.bfloat16)
    minibatch_share = jnp.dot(
        minibatch_normalized_probability, loop_block, preferred_element_type=jnp.float32
    )
    difficult_share = jnp.einsum(
        "qh,qhd->qd",
        tough_candidate_likelihood,
        tough_candidate_tile,
        preferred_element_type=jnp.float32,
    )
    loss_slope_by_question = (
        logit_scaling_coefficient * (minibatch_share + difficult_share)
    ).astype(jnp.bfloat16)
    loop_grad = lax.psum_scatter(
        (
            logit_scaling_coefficient
            * lax.dot_general(
                minibatch_normalized_probability,
                queries,
                (((0,), (0,)), ((), ())),
                preferred_element_type=jnp.float32,
            )
        ).astype(jnp.bfloat16),
        "blk",
        scatter_dimension=0,
        tiled=True,
    ).astype(jnp.float32)
    location_offsets = (
        logit_scaling_coefficient
        * tough_candidate_likelihood.astype(jnp.float32)[:, :, None]
        * queries.astype(jnp.float32)[:, None, :]
    ).astype(jnp.bfloat16)
    location_offsets = location_offsets.reshape(seat_total_number, embedding_width)
    outgoing = (
        jnp.zeros((group_count * capacity, embedding_width), jnp.bfloat16)
        .at[seat_index]
        .set(location_offsets)
    )
    outgoing = outgoing.reshape(group_count, capacity, embedding_width)
    incoming = lax.all_to_all(outgoing, "grp", split_axis=0, concat_axis=0, tiled=True)
    valid_mask = (asked_rows > 0)[:, :, None]
    values = jnp.where(valid_mask, incoming.astype(jnp.float32), 0.0).reshape(-1, embedding_width)
    hard_grad = (
        jnp.zeros((own_rows, embedding_width), jnp.float32)
        .at[jnp.maximum(asked_rows - 1, 0).reshape(-1)]
        .add(values)
    )
    grad_passages = (loop_grad + hard_grad).astype(jnp.bfloat16)
    return (loss, loss_slope_by_question, grad_passages)


def solution(mesh):
    return jax.shard_map(
        shards,
        mesh=mesh,
        in_specs=(
            P(("blk", "grp"), None),
            P(("blk", "grp"), None),
            P(("blk", "grp")),
            P(("blk", "grp"), None),
        ),
        out_specs=(P(), P(("blk", "grp"), None), P(("blk", "grp"), None)),
        check_vma=False,
    )
```

profile of v0, /device:TPU:0, one launch (start us, length us, event | category | flops | bytes accessed | tf_op | source)
XLA Modules:
  0.0 590.5 jit_solution(13337560089130649303)
XLA Ops:
  7.2 0.7 all-gather.2.cloned.1.call-update
  7.9 0.7 and_select_fusion
  8.6 1.2 reduce-window.6
  9.8 0.2 slice_reduce_fusion
  10.0 0.1 fusion.11
  10.1 0.7 fusion.14
  10.8 0.7 compare_select_fusion
  11.5 2.4 scatter_custom_fusion
  14.0 0.1 all_to_all.12
  14.1 22.5 %all_to_all.19 = s32[16,1,64]{2,1,0:T(1,128)S(1)} all-to-all(s32[16,1,64]{2,1,0:T(1,128)S(1)} %all_to_all.12), channel_id=1, replica_groups=mesh['blk'=8,'grp'=16] {'grp'}, dimensions={0} | all-to-all | bytes 8192 | tf_op jit(solution)/shard_map/all_to_all | solution.py:27
  36.6 0.1 reshape.142
  36.7 7.7 %gather_fusion = bf16[1024,4096]{1,0:T(8,128)(2,1)} fusion(bf16[128,4096]{1,0:T(8,128)(2,1)S(1)} %copy-done, s32[1024]{0:T(1024)S(1)} %broadcast_clamp_fusion), kind=kCustom, calls=%fused_computation | custom fusion | bytes 16781312 | tf_op jit(solution)/shard_map/jit(_take)/gather | solution.py:28
  44.4 7.4 %select_select_fusion = bf16[16,64,4096]{2,1,0:T(8,128)(2,1)} fusion(bf16[16,64,4096]{2,1,0:T(8,128)(2,1)} %bitcast.43, pred[16,64]{1,0:T(8,128)(4,1)S(1)} %get-tuple-element.9, pred[16,64]{1,0:T(8,128)(4,1)S(1)} %get-tuple-element.8), kind=kLoop, calls=%fused_computation.15 | loop fusion | flops 8388608 | bytes 16779264 | tf_op jit(solution)/shard_map/jit(_where)/select_n | solution.py:29
  51.9 4.7 all-to-all-start.1
  56.6 0.2 reduce-scatter.2.cloned.1.call-start
  56.8 136.9 %all-to-all-done.1 = bf16[16,64,4096]{2,1,0:T(8,128)(2,1)} async-done(((bf16[16,64,4096]{2,1,0:T(8,128)(2,1)}), bf16[16,64,4096]{2,1,0:T(8,128)(2,1)}, u32[]{:S(2)}, u32[]{:S(2)}) %all-to-all-start.1) | async-done | bytes 8388640 | tf_op jit(solution)/shard_map/all_to_all | solution.py:30
  193.8 13.0 %gather_fusion.1 = bf16[512,4096]{1,0:T(8,128)(2,1)} fusion(bf16[1024,4096]{1,0:T(8,128)(2,1)} %bitcast.11, s32[1024]{0:T(1024)S(1)} %pad_clamp_fusion), kind=kCustom, calls=%fused_computation.1 | custom fusion | bytes 8390656 | tf_op jit(solution)/shard_map/gather | solution.py:31
  206.8 4.7 fusion.1
  211.5 59.0 %all-gather.2.cloned.1.call-done = bf16[1024,4096]{1,0:T(8,128)(2,1)} async-done(((bf16[128,4096]{1,0:T(8,128)(2,1)}), bf16[1024,4096]{1,0:T(8,128)(2,1)}) %all-gather.2.cloned.1.call-update) | async-done | bytes 8388624 | tf_op jit(solution)/shard_map/all_gather | solution.py:14
  270.5 9.3 %multiply_reduce_fusion = (f32[512]{0:T(512)S(1)}, f32[512,1024]{1,0:T(8,128)S(1)}) fusion(bf16[512,4096]{1,0:T(8,128)(2,1)} %param.4, bf16[1024,4096]{1,0:T(8,128)(2,1)} %all-gather.2.cloned.1.call-done), kind=kOutput, calls=%fused_computation.23 | convolution fusion | flops 4296015360 | bytes 14682112 | tf_op jit(solution)/shard_map/dot_general | solution.py:33
  279.9 0.9 select_reduce_fusion
  280.8 7.7 %multiply_convert_fusion = bf16[1024,4096]{1,0:T(8,128)(2,1)} fusion(bf16[512,4096]{1,0:T(8,128)(2,1)S(1)} %copy-done.1, f32[512,1024]{1,0:T(8,128)S(1)} %get-tuple-element.11, f32[512]{0:T(512)S(1)} %get-tuple-element.7, s32[512]{0:T(512)S(1)} %copy-done.2), kind=kOutput, calls=%fused_computation.6 | convolution fusion | flops 4306501632 | bytes 14684160 | tf_op jit(solution)/shard_map/dot_general | solution.py:73
  288.5 12.9 %scatter_custom_fusion.1 = bf16[1024,4096]{1,0:T(8,128)(2,1)} fusion(s32[512]{0:T(512)S(1)} %bitcast.52, bf16[512,4096]{1,0:T(8,128)(2,1)} %param.4, f32[512]{0:T(512)S(1)} %get-tuple-element.5, bf16[]{:T(256)} %constant.74.clone.1), kind=kCustom, calls=%fused_computation.16 | custom fusion | flops 6291456 | bytes 12584962 | tf_op jit(solution)/shard_map/scatter | solution.py:93
  301.3 6.7 %all-to-all-start.2 = ((bf16[16,64,4096]{2,1,0:T(8,128)(2,1)}), bf16[16,64,4096]{2,1,0:T(8,128)(2,1)}, u32[]{:S(2)}, u32[]{:S(2)}) async-start(bf16[16,64,4096]{2,1,0:T(8,128)(2,1)} %bitcast.44), calls=%async_computation.3 | async-start | bytes 16777216 | tf_op jit(solution)/shard_map/all_to_all | solution.py:96
  308.0 0.6 subtract_reduce_fusion
  308.6 217.1 %psum.7 = f32[]{:T(128)} all-reduce(f32[]{:T(128)} %subtract_reduce_fusion), channel_id=1, replica_groups=mesh['blk'=8,'grp'=16] {'blk','grp'}, use_global_device_ids=true, to_apply=%region_8.9 | all-reduce | flops 1 | bytes 8 | tf_op jit(solution)/shard_map/psum | solution.py:50
  526.4 10.6 %fusion.4 = bf16[512,4096]{1,0:T(8,128)(2,1)} fusion(bf16[512,4096]{1,0:T(8,128)(2,1)} %gather_fusion.1, bf16[1024,4096]{1,0:T(8,128)(2,1)} %all-gather.2.cloned.1.call-done, f32[512]{0:T(512)S(1)} %get-tuple-element.6, f32[512,1024]{1,0:T(8,128)S(1)} %get-tuple-element.11, f32[512]{0:T(512)S(1)} %get-tuple-element.7, s32[512]{0:T(512)S(1)} %copy-done.2), kind=kOutput, calls=%fused_computation.14 | convolution fusion | flops 4308598784 | bytes 18880512 | tf_op jit(solution)/shard_map/dot_general | solution.py:58
  537.0 12.0 %convert_select_fusion = f32[16,64,4096]{2,1,0:T(8,128)} fusion(bf16[16,64,4096]{2,1,0:T(8,128)(2,1)} %all-to-all-done.2, pred[16,64]{1,0:T(8,128)(4,1)S(1)} %get-tuple-element.8), kind=kLoop, calls=%fused_computation.5 | loop fusion | flops 8388608 | bytes 25166848 | tf_op jit(solution)/shard_map/jit(_where)/select_n | solution.py:98
  548.9 3.3 reduce-scatter.2.cloned.1.call-done
  552.2 1.4 convert_element_type.48
  553.6 27.6 %scatter_fusion = f32[128,4096]{1,0:T(8,128)S(1)} fusion(f32[128,4096]{1,0:T(8,128)S(1)} %convert_element_type.48, s32[1024]{0:T(1024)S(1)} %reshape.142, f32[1024,4096]{1,0:T(8,128)} %bitcast.42), kind=kCustom, calls=%fused_computation.4 | custom fusion | flops 4194304 | bytes 50335744 | tf_op jit(solution)/shard_map/scatter-add | solution.py:102
  581.2 1.1 convert_element_type.52
  (18 shorter events, 0.2 us)
Async XLA Ops:
  7.2 29.5 %copy-start = (bf16[128,4096]{1,0:T(8,128)(2,1)S(1)}, bf16[128,4096]{1,0:T(8,128)(2,1)}, u32[]{:S(2)}) copy-start(bf16[128,4096]{1,0:T(8,128)(2,1)} %param.5) | copy-start | bytes 3145732
  7.2 263.3 %all-gather.2.cloned.1.call-start = ((), (), s32[]{:S(2)}) async-start(), calls=%async_computation.4 | async-start | bytes 9437184 | tf_op jit(solution)/shard_map/all_gather | solution.py:14
  51.9 141.9 %all-to-all-start.1 = ((bf16[16,64,4096]{2,1,0:T(8,128)(2,1)}), bf16[16,64,4096]{2,1,0:T(8,128)(2,1)}, u32[]{:S(2)}, u32[]{:S(2)}) async-start(bf16[16,64,4096]{2,1,0:T(8,128)(2,1)} %select_select_fusion), calls=%async_computation.1 | async-start | bytes 16777216 | tf_op jit(solution)/shard_map/all_to_all | solution.py:30
  56.6 495.6 %reduce-scatter.2.cloned.1.call-start = ((), (), s32[]{:S(2)}) async-start(), calls=%async_computation.5 | async-start | bytes 9437184 | tf_op jit(solution)/shard_map/reduce_scatter | solution.py:70
  211.5 68.4 %copy-start.2 = (s32[512]{0:T(512)S(1)}, s32[512]{0:T(512)}, u32[]{:S(2)}) copy-start(s32[512]{0:T(512)} %param.6) | copy-start | bytes 6148
  270.5 10.3 %copy-start.1 = (bf16[512,4096]{1,0:T(8,128)(2,1)S(1)}, bf16[512,4096]{1,0:T(8,128)(2,1)}, u32[]{:S(2)}) copy-start(bf16[512,4096]{1,0:T(8,128)(2,1)} %param.4) | copy-start | bytes 12582916
  301.3 235.6 %all-to-all-start.2 = ((bf16[16,64,4096]{2,1,0:T(8,128)(2,1)}), bf16[16,64,4096]{2,1,0:T(8,128)(2,1)}, u32[]{:S(2)}, u32[]{:S(2)}) async-start(bf16[16,64,4096]{2,1,0:T(8,128)(2,1)} %bitcast.44), calls=%async_computation.3 | async-start | bytes 16777216 | tf_op jit(solution)/shard_map/all_to_all | solution.py:96
Sparse Core Ops, SparseCore 0:
  9.7 260.8 all-gather.1
  288.6 263.5 reduce-scatter.1
where the time goes:
time: 600 us; the launch traced here: 590 us
  blocking collectives  240 us (40%)
  waiting for transfers between devices  200 us (33%)
  other arithmetic  71.9 us (12%)
  matrix products  27.6 us (5%)
  local copies, waits for them, and re-layouts  23.6 us (4%)
  between operations  16.1 us (3%)
  starting transfers between devices  11.7 us (2%)
    psum x1, blocking collectives, shards(): loss_sum = lax.psum(jnp.sum(log_total - positive_logit), ('blk', 'grp'))  217 us
    all_to_all x1, waiting for transfers between devices, shards(): lax.all_to_all(picked, 'grp', split_axis=0, concat_axis=0, tiled=True)  137 us
    all_gather x1, waiting for transfers between devices, shards(): loop_block = lax.all_gather(passages, 'blk', axis=0, tiled=True)  59 us
    scatter-add x1, other arithmetic, shards(): hard_grad = jnp.zeros((own_rows, embedding_width), jnp.float32).at[jnp.ma...  27.6 us
    all_to_all x1, blocking collectives, shards(): lax.all_to_all(request, 'grp', split_axis=0, concat_axis=0, tiled=True)  22.5 us
    gather x1, local copies, waits for them, and re-layouts, shards(): returned.reshape(group_count * capacity, embedding_width)[seat_index]  13 us
    scatter x1, other arithmetic, shards(): outgoing = jnp.zeros((group_count * capacity, embedding_width), jnp.bfloa...  12.9 us
  transfers between devices with their start and end apart: 4, of which 3 were waited for; matrix products, arithmetic and copies ran while one was open for 13% of the time, Pallas kernels for 0%

commit v1 on v0

v1 whole, which is shorter than its diff:
```python
import functools

import jax
import jax.numpy as jnp
from jax import lax
from jax.experimental import pallas as pl
from jax.experimental.pallas import tpu as pltpu
from jax.sharding import PartitionSpec as P

logit_scaling_coefficient = 20.0
MESH = pl.DeviceIdType.MESH
BF16 = jnp.bfloat16
F32 = jnp.float32
COPIES = 80
NT = (((1,), (1,)), ((), ()))


def rows(start, size, multiple=64):
    return pl.ds(pl.multiple_of(start, multiple), size)


def kernel(
    q_hbm, p_hbm, pos_ref, hid_ref,
    loss_ref, dq_hbm, dp_hbm, other_hbm,
    lbuf, pbuf, qbuf, s, wt, wall, wht, xs, ys, xrf, xrs, yrf, yrs, zrh, zrl,
    ids, hs, hin, w2, top, lsum, lsend, lrecv, otile, dqt,
    ssem, rsem, csem,
):
    q_dev, width = q_hbm.shape
    p_dev = p_hbm.shape[0]
    half = p_dev // 2
    scale = logit_scaling_coefficient

    b = lax.axis_index("blk")
    g = lax.axis_index("grp")
    x, zl = lax.div(b, 2), lax.rem(b, 2)
    zh, y, core = lax.div(g, 8), lax.div(lax.rem(g, 8), 2), lax.rem(g, 2)
    pb = x * 2 + 1 - zl
    px = [lax.rem(x + k, 4) for k in range(4)]
    py = [lax.rem(y + k, 4) for k in range(4)]
    xp = (px[1] * 2 + zl, g)
    xm = (px[3] * 2 + zl, g)
    yp = (b, zh * 8 + py[1] * 2 + core)
    ym = (b, zh * 8 + py[3] * 2 + core)
    p1 = (pb, g)
    p2 = (pb, lax.rem(g + 8, 16))
    sib = (b, zh * 8 + y * 2 + 1 - core)

    number = {}
    started = {}

    def describe(name, src, dst, peer):
        k = number.setdefault(name, len(number))
        return pltpu.make_async_remote_copy(
            src_ref=src, dst_ref=dst, send_sem=ssem.at[k], recv_sem=rsem.at[k],
            device_id=peer, device_id_type=MESH,
        )

    def send(name, src, dst, peer):
        copy = describe(name, src, dst, peer)
        copy.start()
        started[name] = copy

    def sent(name):
        started.pop(name).wait_send()

    def arrived(name, dst):
        describe(name, dst, dst, sib).wait_recv()

    barrier = pltpu.get_barrier_semaphore()
    for peer in (xp, xm, yp, ym, p1, p2, sib):
        pl.semaphore_signal(barrier, inc=1, device_id=peer, device_id_type=MESH)
    pl.semaphore_wait(barrier, 7)

    def lrow(xx, zz, h=0, n=p_dev):
        return lbuf.at[rows((xx * 2 + zz) * p_dev + h * half, n)]

    def prow(yy, zz, h=0, n=p_dev):
        return pbuf.at[rows((yy * 2 + zz) * p_dev + h * half, n)]

    def orow(yy, zz):
        return other_hbm.at[rows((yy * 2 + zz) * p_dev, p_dev)]

    own = [p_hbm.at[pl.ds(h * half, half)] for h in range(2)]

    for h in range(2):
        send(f"z{h}", own[h], lrow(x, zl, h, half), p1)
    for h in range(2):
        send(f"x+o{h}", own[h], lrow(x, zl, h, half), xp)
        send(f"x-o{1 - h}", own[1 - h], lrow(x, zl, 1 - h, half), xm)
        send(f"y+o{h}", own[h], prow(y, zh, h, half), yp)
        send(f"y-o{1 - h}", own[1 - h], prow(y, zh, 1 - h, half), ym)
    local = [
        pltpu.make_async_copy(q_hbm, qbuf.at[pl.ds(0, q_dev)], csem.at[0]),
        pltpu.make_async_copy(p_hbm, lrow(x, zl), csem.at[1]),
        pltpu.make_async_copy(p_hbm, prow(y, zh), csem.at[2]),
    ]
    for copy in local:
        copy.start()
    ids[0] = jnp.broadcast_to(hid_ref[...], ids.shape[1:])
    send("ids", ids.at[0], ids.at[1], sib)
    send("q", q_hbm, qbuf.at[pl.ds(q_dev, q_dev)], sib)
    send("oo", p_hbm, orow(y, zh), sib)

    hs[...] = jnp.zeros(hs.shape, F32)
    top[...] = jnp.full(top.shape, -jnp.inf, F32)

    def score_loop(xx, zz):
        c = xx * 2 + zz

        @pl.loop(0, q_dev // 256)
        def _(n):
            cols = rows(n * 256, 256, 256)
            acc = scale * lax.dot_general(
                lbuf[rows(c * p_dev, p_dev), :], qbuf[cols, :], NT, preferred_element_type=F32
            )
            s[:, rows(c * q_dev + n * 256, 256, 256)] = acc
            top[:, cols] = jnp.maximum(top[:, cols], jnp.max(acc, axis=0, keepdims=True))

    def pool_base(yy, zz, cc):
        return (zz * 8 + yy * 2 + cc) * p_dev

    def score_pool(yy, zz):
        slot = yy * 2 + zz
        base = pool_base(yy, zz, core)
        for k in range(2):

            @pl.loop(0, q_dev // 256)
            def _(n):
                cols = rows(n * 256, 256, 256)
                acc = lax.dot_general(
                    pbuf[rows(slot * p_dev, p_dev), :],
                    qbuf[rows(k * q_dev + n * 256, 256, 256), :],
                    NT,
                    preferred_element_type=F32,
                )
                row = lax.broadcasted_iota(jnp.int32, acc.shape, 0) + base
                named = jnp.where(row == ids[k, 0:1, cols], scale * acc, 0.0)
                hs[k, :, cols] += jnp.sum(named, axis=0, keepdims=True)

    oz, oh = 1 - zl, 1 - zh

    for copy in local:
        copy.wait()
    score_loop(x, zl)

    arrived("x+o0", lrow(px[3], zl, 0, half))
    send("x+f", lrow(px[3], zl, 0, half), lrow(px[3], zl, 0, half), xp)
    arrived("x-o1", lrow(px[1], zl, 1, half))
    send("x-f", lrow(px[1], zl, 1, half), lrow(px[1], zl, 1, half), xm)
    arrived("y+o0", prow(py[3], zh, 0, half))
    send("y+f", prow(py[3], zh, 0, half), prow(py[3], zh, 0, half), yp)
    arrived("y-o1", prow(py[1], zh, 1, half))
    send("y-f", prow(py[1], zh, 1, half), prow(py[1], zh, 1, half), ym)
    arrived("z0", lrow(x, oz, 0, half))
    send("h0", lrow(x, oz, 0, half), prow(y, zh, 0, half), p2)
    send("x+p0", lrow(x, oz, 0, half), lrow(x, oz, 0, half), xp)
    arrived("ids", ids.at[1])
    arrived("q", qbuf.at[pl.ds(q_dev, q_dev)])
    score_pool(y, zh)

    arrived("z1", lrow(x, oz, 1, half))
    send("h1", lrow(x, oz, 1, half), prow(y, zh, 1, half), p2)
    send("x-p1", lrow(x, oz, 1, half), lrow(x, oz, 1, half), xm)
    send("x+p1", lrow(x, oz, 1, half), lrow(x, oz, 1, half), xp)
    send("x-p0", lrow(x, oz, 0, half), lrow(x, oz, 0, half), xm)
    arrived("h0", prow(y, oh, 0, half))
    send("y+p0", prow(y, oh, 0, half), prow(y, oh, 0, half), yp)
    score_loop(x, oz)
    arrived("x+o1", lrow(px[3], zl, 1, half))
    score_loop(px[3], zl)
    arrived("x-o0", lrow(px[1], zl, 0, half))
    score_loop(px[1], zl)
    arrived("y+o1", prow(py[3], zh, 1, half))
    send("o3", prow(py[3], zh), orow(py[3], zh), sib)
    score_pool(py[3], zh)
    arrived("y-o0", prow(py[1], zh, 0, half))
    send("o1", prow(py[1], zh), orow(py[1], zh), sib)
    arrived("h1", prow(y, oh, 1, half))
    send("y-p1", prow(y, oh, 1, half), prow(y, oh, 1, half), ym)
    send("y+p1", prow(y, oh, 1, half), prow(y, oh, 1, half), yp)
    send("y-p0", prow(y, oh, 0, half), prow(y, oh, 0, half), ym)
    send("op", prow(y, oh), orow(y, oh), sib)
    score_pool(py[1], zh)
    arrived("x+f", lrow(px[2], zl, 0, half))
    arrived("x-f", lrow(px[2], zl, 1, half))
    score_loop(px[2], zl)
    arrived("y+f", prow(py[2], zh, 0, half))
    arrived("y-f", prow(py[2], zh, 1, half))
    send("o2", prow(py[2], zh), orow(py[2], zh), sib)
    arrived("x+p0", lrow(px[3], oz, 0, half))
    send("x+g", lrow(px[3], oz, 0, half), lrow(px[3], oz, 0, half), xp)
    arrived("x-p1", lrow(px[1], oz, 1, half))
    send("x-g", lrow(px[1], oz, 1, half), lrow(px[1], oz, 1, half), xm)
    arrived("y+p0", prow(py[3], oh, 0, half))
    send("y+g", prow(py[3], oh, 0, half), prow(py[3], oh, 0, half), yp)
    arrived("y-p1", prow(py[1], oh, 1, half))
    send("y-g", prow(py[1], oh, 1, half), prow(py[1], oh, 1, half), ym)
    score_pool(y, oh)
    score_pool(py[2], zh)
    arrived("x+p1", lrow(px[3], oz, 1, half))
    score_loop(px[3], oz)
    arrived("x-p0", lrow(px[1], oz, 0, half))
    score_loop(px[1], oz)
    arrived("y+p1", prow(py[3], oh, 1, half))
    score_pool(py[3], oh)
    arrived("y-p0", prow(py[1], oh, 0, half))
    score_pool(py[1], oh)
    arrived("y+g", prow(py[2], oh, 0, half))
    arrived("y-g", prow(py[2], oh, 1, half))
    score_pool(py[2], oh)
    send("hs", hs.at[1], hin, sib)
    arrived("x+g", lrow(px[2], oz, 0, half))
    arrived("x-g", lrow(px[2], oz, 1, half))
    score_loop(px[2], oz)

    arrived("hs", hin)
    hard = hs[0] + hin[...]
    hard = hard[0:1]
    peak = jnp.maximum(top[0:1], hard)
    total = jnp.exp(hard - peak)
    positive = jnp.zeros_like(peak)
    blocks = s.shape[1] // q_dev
    for c in range(blocks):
        part = s[:, c * q_dev:(c + 1) * q_dev]
        total += jnp.sum(jnp.exp(part - peak), axis=0, keepdims=True)
        row = lax.broadcasted_iota(jnp.int32, part.shape, 0) + c * p_dev
        positive += jnp.sum(jnp.where(row == pos_ref[...], part, 0.0), axis=0, keepdims=True)
    log_total = peak + jnp.log(total)
    w_hard = jnp.exp(hard - log_total).astype(BF16).astype(F32)
    w2[0] = jnp.broadcast_to(w_hard, w2.shape[1:])
    send("w", w2.at[0], w2.at[1], sib)
    for c in range(blocks):
        part = s[:, c * q_dev:(c + 1) * q_dev]
        row = lax.broadcasted_iota(jnp.int32, part.shape, 0) + c * p_dev
        hit = jnp.where(row == pos_ref[...], 1.0, 0.0)
        wt[c * p_dev:(c + 1) * p_dev, :] = (jnp.exp(part - log_total) - hit).astype(BF16)
    lsum[...] = jnp.broadcast_to(
        jnp.sum(log_total - positive, axis=1, keepdims=True), lsum.shape
    )

    x_pair = [
        (lax.rem(b + 2 + 4 * lax.rem(x, 2), 8), g),
        ((3 - x) * 2 + zl, g),
    ]
    y_pair = [
        (b, zh * 8 + lax.rem(y + 1 + 2 * lax.rem(y, 2), 4) * 2 + core),
        (b, zh * 8 + (3 - y) * 2 + core),
    ]
    loss_peers = [x_pair[0], y_pair[0], x_pair[1], y_pair[1], p1, p2, sib]

    def loss_start(k):
        lsend[k] = lsum[...]
        send(f"l{k}", lsend.at[k], lrecv.at[k], loss_peers[k])

    def loss_finish(k):
        arrived(f"l{k}", lrecv.at[k])
        lsum[...] = lsend[k] + lrecv[k]

    step = 512

    def loop_part(start, count, store):
        @pl.loop(0, width // step)
        def _(t):
            cols = rows(t * step, step, step)
            store(cols, scale * jnp.dot(
                wt[rows(start, count), :], qbuf[pl.ds(0, q_dev), cols],
                preferred_element_type=F32,
            ))

    def pool_weights(yy, zz, at):
        base = pool_base(yy, zz, core)
        for k in range(2):
            row = lax.broadcasted_iota(jnp.int32, (p_dev, q_dev), 0) + base
            wht[at:at + p_dev, k * q_dev:(k + 1) * q_dev] = jnp.where(
                row == ids[k, 0:1, :], w2[k, 0:1, :], 0.0
            ).astype(BF16)

    def pool_part(count, store):
        @pl.loop(0, width // step)
        def _(t):
            cols = rows(t * step, step, step)
            store(cols, scale * jnp.dot(
                wht[pl.ds(0, count), :], qbuf[:, cols], preferred_element_type=F32
            ))

    def into(ref, k):
        def store(cols, value):
            ref[k, :, cols] = value.astype(BF16)
        return store

    def x_part(k):
        slot = {1: 0, 3: 1, 2: 2}[k]
        loop_part(px[k] * 2 * p_dev, 2 * p_dev, into(xs, slot))

    def y_part(k):
        slot = {1: 0, 3: 1, 2: 2}[k]
        pool_weights(py[k], 0, 0)
        pool_weights(py[k], 1, p_dev)
        pool_part(2 * p_dev, into(ys, slot))

    z_of = {"x": (oz, zl), "y": (oh, zh)}
    axes = {"x": (xs, xrf, xrs, xp, xm), "y": (ys, yrf, yrs, yp, ym)}

    def piece(a, slot, role, h, n=half):
        return axes[a][0].at[slot, rows(z_of[a][role] * p_dev + h * half, n)]

    def send_far(a, role):
        _, rf, _, plus, minus = axes[a]
        send(f"{a}+s2{role}", piece(a, 2, role, 0), rf.at[0, role], plus)
        send(f"{a}-s2{role}", piece(a, 2, role, 1), rf.at[1, role], minus)

    def send_near(a, role):
        _, _, rs, plus, minus = axes[a]
        send(f"{a}+s1{role}", piece(a, 0, role, 1), rs.at[0, role, pl.ds(half, half)], plus)
        send(f"{a}-s1{role}", piece(a, 1, role, 0), rs.at[1, role, pl.ds(0, half)], minus)

    def send_sum(a, role):
        _, rf, rs, plus, minus = axes[a]
        for d, (sign, slot, h, peer) in enumerate((("+", 0, 0, plus), ("-", 1, 1, minus))):
            arrived(f"{a}{sign}s2{role}", rf.at[d, role])
            mine = piece(a, slot, role, h)

            @pl.loop(0, width // step)
            def _(t):
                cols = rows(t * step, step, step)
                mine[:, cols] = (
                    mine[:, cols].astype(F32) + rf[d, role, :, cols].astype(F32)
                ).astype(BF16)

            send(f"{a}{sign}s0{role}", mine, rs.at[d, role, pl.ds(h * half, half)], peer)

    def sums_arrived(a, role):
        rs = axes[a][2]
        for d, sign in enumerate("+-"):
            near = 1 - d
            arrived(f"{a}{sign}s1{role}", rs.at[d, role, pl.ds(near * half, half)])
            arrived(f"{a}{sign}s0{role}", rs.at[d, role, pl.ds(d * half, half)])

    x_part(2)
    send_far("x", 0)
    arrived("w", w2.at[1])
    loss_start(0)
    y_part(2)
    send_far("y", 0)
    send("o4", prow(py[3], oh), orow(py[3], oh), sib)
    send("o5", prow(py[1], oh), orow(py[1], oh), sib)
    send("o6", prow(py[2], oh), orow(py[2], oh), sib)
    x_part(1)
    x_part(3)
    send_near("x", 0)
    loss_finish(0)
    loss_start(1)
    y_part(1)
    y_part(3)
    send_near("y", 0)
    send_sum("x", 0)
    send_sum("y", 0)
    send_far("x", 1)
    send_far("y", 1)
    send_near("x", 1)
    send_near("y", 1)
    loss_finish(1)
    loss_start(2)

    for a in "xy":
        sent(f"{a}+s20")
        sent(f"{a}-s20")

    hand_x = xs.at[2, rows(oz * p_dev, p_dev)]
    hand_y = ys.at[2, rows(oh * p_dev, p_dev)]

    def store_hand_x(cols, value):
        hand_x[:, cols] = value.astype(BF16)

    def store_hand_y(cols, value):
        hand_y[:, cols] = value.astype(BF16)

    def store_own(cols, value):
        s[:, cols] = value

    def add_own(cols, value):
        s[:, cols] += value

    pool_weights(y, oh, 0)
    pool_part(p_dev, store_hand_y)
    loop_part((x * 2 + oz) * p_dev, p_dev, store_hand_x)
    loop_part((x * 2 + zl) * p_dev, p_dev, store_own)
    pool_weights(y, zh, 0)
    pool_part(p_dev, add_own)
    loss_finish(2)
    loss_start(3)

    for c in range(blocks):
        wall[:, c * p_dev:(c + 1) * p_dev] = (
            wt[c * p_dev:(c + 1) * p_dev, :].astype(F32).T.astype(BF16)
        )
    loop_rows = blocks * p_dev

    @pl.loop(0, q_dev // 128)
    def _(n):
        part = rows(n * 128, 128, 128)
        names = jnp.broadcast_to(ids[0, 0:1, part].astype(F32), (128, 128)).T
        values = jnp.broadcast_to(w2[0, 0:1, part], (128, 128)).T
        lane = lax.broadcasted_iota(jnp.int32, (128, 128), 1)
        for k in range(2):
            cc = core if k == 0 else 1 - core
            for slot in range(8):
                base = pool_base(slot // 2, slot % 2, cc)
                at = loop_rows + (k * 8 + slot) * p_dev
                wall[part, at:at + p_dev] = jnp.where(
                    names == (lane + base).astype(F32), values, 0.0
                ).astype(BF16)

    arrived("oo", orow(y, zh))
    arrived("o3", orow(py[3], zh))
    arrived("o1", orow(py[1], zh))
    arrived("op", orow(y, oh))
    arrived("o2", orow(py[2], zh))
    arrived("o4", orow(py[3], oh))
    arrived("o5", orow(py[1], oh))
    arrived("o6", orow(py[2], oh))

    tile = dqt.shape[2]
    tiles = width // tile
    pool_rows = pbuf.shape[0]

    def tile_in(t):
        k = lax.rem(t, 2)
        return pltpu.make_async_copy(
            other_hbm.at[:, rows(t * tile, tile, tile)], otile.at[k], csem.at[k]
        )

    def tile_out(t):
        k = lax.rem(t, 2)
        return pltpu.make_async_copy(
            dqt.at[k], dq_hbm.at[:, rows(t * tile, tile, tile)], csem.at[2 + k]
        )

    tile_in(0).start()

    def query_slope(first, last):
        @pl.loop(first, last)
        def _(t):
            k = lax.rem(t, 2)

            @pl.when(t + 1 < tiles)
            def _():
                tile_in(t + 1).start()

            @pl.when(t >= 2)
            def _():
                tile_out(t - 2).wait()

            cols = rows(t * tile, tile, tile)
            tile_in(t).wait()
            acc = jnp.dot(
                wall[:, 0:loop_rows], lbuf[:, cols], preferred_element_type=F32
            )
            acc += jnp.dot(
                wall[:, loop_rows:loop_rows + pool_rows], pbuf[:, cols],
                preferred_element_type=F32,
            )
            acc += jnp.dot(
                wall[:, loop_rows + pool_rows:], otile[k], preferred_element_type=F32
            )
            dqt[k] = (scale * acc).astype(BF16)
            tile_out(t).start()

    query_slope(0, tiles // 4)
    loss_finish(3)
    loss_start(4)
    query_slope(tiles // 4, tiles // 2)

    sums_arrived("y", 0)
    for h in range(2):
        part = pl.ds(h * half, half)

        @pl.loop(0, width // step)
        def _(t):
            cols = rows(t * step, step, step)
            hand_y[part, cols] = (
                hand_y[part, cols].astype(F32)
                + yrs[0, 0, part, cols].astype(F32)
                + yrs[1, 0, part, cols].astype(F32)
            ).astype(BF16)

        send(f"zh{h}", hand_y.at[part], zrh.at[part], p2)
    loss_finish(4)
    loss_start(5)
    query_slope(tiles // 2, tiles * 3 // 4)
    send_sum("x", 1)
    send_sum("y", 1)
    loss_finish(5)
    loss_start(6)
    sums_arrived("x", 0)
    for h in range(2):
        part = pl.ds(h * half, half)
        arrived(f"zh{h}", zrh.at[part])

        @pl.loop(0, width // step)
        def _(t):
            cols = rows(t * step, step, step)
            hand_x[part, cols] = (
                hand_x[part, cols].astype(F32)
                + xrs[0, 0, part, cols].astype(F32)
                + xrs[1, 0, part, cols].astype(F32)
                + zrh[part, cols].astype(F32)
            ).astype(BF16)

        send(f"zl{h}", hand_x.at[part], zrl.at[part], p1)
    query_slope(tiles * 3 // 4, tiles)
    loss_finish(6)
    loss_ref[...] = lsum[...]

    sums_arrived("x", 1)
    sums_arrived("y", 1)
    sent("y+s21")
    sent("y-s21")
    result = ys.at[2, rows(zh * p_dev, p_dev)]
    outs = []
    for h in range(2):
        part = pl.ds(h * half, half)
        arrived(f"zl{h}", zrl.at[part])

        @pl.loop(0, width // step)
        def _(t):
            cols = rows(t * step, step, step)
            result[part, cols] = (
                s[part, cols]
                + xrs[0, 1, part, cols].astype(F32)
                + xrs[1, 1, part, cols].astype(F32)
                + yrs[0, 1, part, cols].astype(F32)
                + yrs[1, 1, part, cols].astype(F32)
                + zrl[part, cols].astype(F32)
            ).astype(BF16)

        copy = pltpu.make_async_copy(result.at[part], dp_hbm.at[part], csem.at[h])
        copy.start()
        outs.append(copy)
    tile_out(tiles - 2).wait()
    tile_out(tiles - 1).wait()
    for copy in outs:
        copy.wait()
    for name in list(started):
        sent(name)


def shards(queries, passages, positive_ids, hard_ids):
    q_dev, width = queries.shape
    p_dev = passages.shape[0]
    half = p_dev // 2
    vmem = pltpu.VMEM
    hbm = pl.BlockSpec(memory_space=pl.ANY)
    block = pl.BlockSpec(memory_space=pltpu.VMEM)
    loss, slope, grad, _ = pl.pallas_call(
        kernel,
        out_shape=(
            jax.ShapeDtypeStruct((8, 128), F32),
            jax.ShapeDtypeStruct((q_dev, width), BF16),
            jax.ShapeDtypeStruct((p_dev, width), BF16),
            jax.ShapeDtypeStruct((8 * p_dev, width), BF16),
        ),
        in_specs=[hbm, hbm, block, block],
        out_specs=(block, hbm, hbm, hbm),
        scratch_shapes=[
            vmem((8 * p_dev, width), BF16),
            vmem((8 * p_dev, width), BF16),
            vmem((2 * q_dev, width), BF16),
            vmem((p_dev, 8 * q_dev), F32),
            vmem((8 * p_dev, q_dev), BF16),
            vmem((q_dev, 24 * p_dev), BF16),
            vmem((2 * p_dev, 2 * q_dev), BF16),
            vmem((3, 2 * p_dev, width), BF16),
            vmem((3, 2 * p_dev, width), BF16),
            vmem((2, 2, half, width), BF16),
            vmem((2, 2, p_dev, width), BF16),
            vmem((2, 2, half, width), BF16),
            vmem((2, 2, p_dev, width), BF16),
            vmem((p_dev, width), BF16),
            vmem((p_dev, width), BF16),
            vmem((2, 8, q_dev), jnp.int32),
            vmem((2, 8, q_dev), F32),
            vmem((8, q_dev), F32),
            vmem((2, 8, q_dev), F32),
            vmem((8, q_dev), F32),
            vmem((8, 128), F32),
            vmem((7, 8, 128), F32),
            vmem((7, 8, 128), F32),
            vmem((2, 8 * p_dev, 256), BF16),
            vmem((2, q_dev, 256), BF16),
            pltpu.SemaphoreType.DMA((COPIES,)),
            pltpu.SemaphoreType.DMA((COPIES,)),
            pltpu.SemaphoreType.DMA((4,)),
        ],
        compiler_params=pltpu.CompilerParams(
            collective_id=0, has_side_effects=True, vmem_limit_bytes=63 * 2**20
        ),
        cost_estimate=pl.CostEstimate(
            flops=2 * q_dev * width * 9 * 8 * p_dev,
            bytes_accessed=40 * 2**20,
            transcendentals=2 * 8 * p_dev * q_dev,
        ),
    )(
        queries,
        passages,
        positive_ids.reshape(1, q_dev),
        hard_ids.reshape(1, q_dev),
    )
    total = q_dev * lax.axis_size("blk") * lax.axis_size("grp")
    return loss[0, 0] / total, slope, grad


def solution(mesh):
    return jax.shard_map(
        shards,
        mesh=mesh,
        in_specs=(
            P(("blk", "grp"), None),
            P(("blk", "grp"), None),
            P(("blk", "grp")),
            P(("blk", "grp"), None),
        ),
        out_specs=(P(), P(("blk", "grp"), None), P(("blk", "grp"), None)),
        check_vma=False,
    )
```

time: 600 us -> 214 us (0.36); the launches traced: 590 us -> 212 us
  blocking collectives: 240 us -> 0 us
  Pallas kernels: 0 us -> 202 us
  waiting for transfers between devices: 200 us -> 0 us
  other arithmetic: 71.9 us -> 0 us
  matrix products: 27.6 us -> 0 us
  local copies, waits for them, and re-layouts: 23.6 us -> 6.95 us
  between operations: 16.1 us -> 2.43 us
  starting transfers between devices: 11.7 us -> 0 us
    psum x1 -> x0, blocking collectives: 217 us -> none  [shards(): loss_sum = lax.psum(jnp.sum(log_total - positive_logit), ('blk', 'grp'))]
    pallas_call x0 -> x1, Pallas kernels: none -> 202 us  [shards(): pl.pallas_call(kernel, out_shape=(jax.ShapeDtypeStruct((8, 128), F32), ja...]
    all_to_all x2 -> x0, waiting for transfers between devices: 137 us -> none  [the longest x1 137 us: shards(): lax.all_to_all(picked, 'grp', split_axis=0, concat_axis=0, tiled=True)]
    all_gather x1 -> x0, waiting for transfers between devices: 59 us -> none  [shards(): loop_block = lax.all_gather(passages, 'blk', axis=0, tiled=True)]
    scatter-add x1 -> x0, other arithmetic: 27.6 us -> none  [shards(): hard_grad = jnp.zeros((own_rows, embedding_width), jnp.float32).at[jnp.ma...]
    dot_general x3 -> x0, matrix products: 27.6 us -> none  [the longest x1 10.6 us: shards(): jnp.dot(minibatch_normalized_probability, loop_block, preferred_element_t...]
    all_to_all x1 -> x0, blocking collectives: 22.5 us -> none  [shards(): lax.all_to_all(request, 'grp', split_axis=0, concat_axis=0, tiled=True)]
    select_n x4 -> x0, other arithmetic: 20.8 us -> none  [the longest x1 12 us: shards(): jnp.where(valid_mask, incoming.astype(jnp.float32), 0.0)]
  transfers between devices with their start and end apart: 4 -> 0, of which waited for: 3 -> 0; matrix products, arithmetic and copies ran while one was open for 13% -> 0% of each run, Pallas kernels for 0% -> 0%
where the time goes in v1:
time: 214 us; the launch traced here: 212 us
  Pallas kernels  202 us (94%)
  local copies, waits for them, and re-layouts  6.95 us (3%)
  between operations  2.43 us (1%)
    pallas_call x1, Pallas kernels, shards(): pl.pallas_call(kernel, out_shape=(jax.ShapeDtypeStruct((8, 128), F32), ja...  202 us
    unnamed x4, local copies, waits for them, and re-layouts  5.76 us

profile of v1, /device:TPU:0, one launch (start us, length us, event | category | flops | bytes accessed | tf_op | source)
XLA Modules:
  0.0 211.5 jit_solution(2385974630131832648)
XLA Ops:
  0.6 202.2 %shard_map.67 = (f32[8,128]{1,0:T(8,128)}, bf16[512,4096]{1,0:T(8,128)(2,1)}, bf16[128,4096]{1,0:T(8,128)(2,1)}, bf16[1024,4096]{1,0:T(8,128)(2,1)}) custom-call(bf16[512,4096]{1,0:T(8,128)(2,1)} %q_hbm.1, bf16[128,4096]{1,0:T(8,128)(2,1)} %p_hbm.1, s32[1,512]{1,0:T(1,128)} %bitcast.3, s32[1,512]{1,0:T(1,128)} %bitcast.4), custom_call_target="tpu_custom_call" | custom-call | flops 38654705664 | bytes 41943040 | tf_op jit(solution)/shard_map/pallas_call | solution.py:556
  202.8 1.2 slice.3
  204.6 0.0 copy-start
  204.6 4.8 %copy.9 = bf16[512,4096]{1,0:T(8,128)(2,1)} copy(bf16[512,4096]{1,0:T(8,128)(2,1)} %get-tuple-element.13) | data formatting | bytes 8388608
  209.4 0.0 copy-done
  209.4 1.0 copy.10
Async XLA Ops:
  204.6 4.8 %copy-start = (bf16[128,4096]{1,0:T(8,128)(2,1)S(1)}, bf16[128,4096]{1,0:T(8,128)(2,1)}, u32[]{:S(2)}) copy-start(bf16[128,4096]{1,0:T(8,128)(2,1)} %get-tuple-element.14) | copy-start | bytes 3145732

commit v2 on v1

--- a/solution.py
+++ b/solution.py
@@ -239,15 +239,15 @@
         jnp.sum(log_total - positive, axis=1, keepdims=True), lsum.shape
     )
 
-    x_pair = [
+    loss_peers = [
         (lax.rem(b + 2 + 4 * lax.rem(x, 2), 8), g),
+        (b, zh * 8 + lax.rem(y + 1 + 2 * lax.rem(y, 2), 4) * 2 + core),
+        p1,
+        p2,
+        sib,
         ((3 - x) * 2 + zl, g),
-    ]
-    y_pair = [
-        (b, zh * 8 + lax.rem(y + 1 + 2 * lax.rem(y, 2), 4) * 2 + core),
         (b, zh * 8 + (3 - y) * 2 + core),
     ]
-    loss_peers = [x_pair[0], y_pair[0], x_pair[1], y_pair[1], p1, p2, sib]
 
     def loss_start(k):
         lsend[k] = lsum[...]
@@ -257,10 +257,12 @@
         arrived(f"l{k}", lrecv.at[k])
         lsum[...] = lsend[k] + lrecv[k]
 
+    loss_start(0)
+
     step = 512
 
     def loop_part(start, count, store):
-        @pl.loop(0, width // step)
+        @pl.loop(0, width // step, unroll=4)
         def _(t):
             cols = rows(t * step, step, step)
             store(cols, scale * jnp.dot(
@@ -277,7 +279,7 @@
             ).astype(BF16)
 
     def pool_part(count, store):
-        @pl.loop(0, width // step)
+        @pl.loop(0, width // step, unroll=4)
         def _(t):
             cols = rows(t * step, step, step)
             store(cols, scale * jnp.dot(
@@ -339,29 +341,34 @@
 
     x_part(2)
     send_far("x", 0)
+    loss_finish(0)
+    loss_start(1)
     arrived("w", w2.at[1])
-    loss_start(0)
     y_part(2)
+    loss_finish(1)
     send_far("y", 0)
+    loss_start(2)
     send("o4", prow(py[3], oh), orow(py[3], oh), sib)
     send("o5", prow(py[1], oh), orow(py[1], oh), sib)
     send("o6", prow(py[2], oh), orow(py[2], oh), sib)
     x_part(1)
     x_part(3)
     send_near("x", 0)
-    loss_finish(0)
-    loss_start(1)
+    loss_finish(2)
+    loss_start(3)
     y_part(1)
     y_part(3)
     send_near("y", 0)
+    loss_finish(3)
+    loss_start(4)
     send_sum("x", 0)
     send_sum("y", 0)
+    loss_finish(4)
+    loss_start(5)
     send_far("x", 1)
     send_far("y", 1)
     send_near("x", 1)
     send_near("y", 1)
-    loss_finish(1)
-    loss_start(2)
 
     for a in "xy":
         sent(f"{a}+s20")
@@ -370,26 +377,24 @@
     hand_x = xs.at[2, rows(oz * p_dev, p_dev)]
     hand_y = ys.at[2, rows(oh * p_dev, p_dev)]
 
-    def store_hand_x(cols, value):
-        hand_x[:, cols] = value.astype(BF16)
-
-    def store_hand_y(cols, value):
-        hand_y[:, cols] = value.astype(BF16)
-
-    def store_own(cols, value):
-        s[:, cols] = value
-
-    def add_own(cols, value):
-        s[:, cols] += value
-
-    pool_weights(y, oh, 0)
-    pool_part(p_dev, store_hand_y)
-    loop_part((x * 2 + oz) * p_dev, p_dev, store_hand_x)
-    loop_part((x * 2 + zl) * p_dev, p_dev, store_own)
-    pool_weights(y, zh, 0)
-    pool_part(p_dev, add_own)
-    loss_finish(2)
-    loss_start(3)
+    def split(first, value):
+        low, high = value[:p_dev], value[p_dev:]
+        return jnp.where(first, low, high), jnp.where(first, high, low)
+
+    def store_x(cols, value):
+        mine, handed = split(zl == 0, value)
+        s[:, cols] = mine
+        hand_x[:, cols] = handed.astype(BF16)
+
+    def store_y(cols, value):
+        mine, handed = split(zh == 0, value)
+        s[:, cols] += mine
+        hand_y[:, cols] = handed.astype(BF16)
+
+    loop_part(x * 2 * p_dev, 2 * p_dev, store_x)
+    pool_weights(y, 0, 0)
+    pool_weights(y, 1, p_dev)
+    pool_part(2 * p_dev, store_y)
 
     for c in range(blocks):
         wall[:, c * p_dev:(c + 1) * p_dev] = (
@@ -467,16 +472,16 @@
             dqt[k] = (scale * acc).astype(BF16)
             tile_out(t).start()
 
-    query_slope(0, tiles // 4)
-    loss_finish(3)
-    loss_start(4)
-    query_slope(tiles // 4, tiles // 2)
-
+    query_slope(0, tiles * 3 // 4)
+    loss_finish(5)
+    loss_start(6)
+
+    quarter = half // 2
+    parts = [pl.ds(k * quarter, quarter) for k in range(4)]
     sums_arrived("y", 0)
-    for h in range(2):
-        part = pl.ds(h * half, half)
-
-        @pl.loop(0, width // step)
+    for k, part in enumerate(parts):
+
+        @pl.loop(0, width // step, unroll=2)
         def _(t):
             cols = rows(t * step, step, step)
             hand_y[part, cols] = (
@@ -485,20 +490,14 @@
                 + yrs[1, 0, part, cols].astype(F32)
             ).astype(BF16)
 
-        send(f"zh{h}", hand_y.at[part], zrh.at[part], p2)
-    loss_finish(4)
-    loss_start(5)
-    query_slope(tiles // 2, tiles * 3 // 4)
+        send(f"zh{k}", hand_y.at[part], zrh.at[part], p2)
+    sums_arrived("x", 0)
     send_sum("x", 1)
     send_sum("y", 1)
-    loss_finish(5)
-    loss_start(6)
-    sums_arrived("x", 0)
-    for h in range(2):
-        part = pl.ds(h * half, half)
-        arrived(f"zh{h}", zrh.at[part])
-
-        @pl.loop(0, width // step)
+    for k, part in enumerate(parts):
+        arrived(f"zh{k}", zrh.at[part])
+
+        @pl.loop(0, width // step, unroll=2)
         def _(t):
             cols = rows(t * step, step, step)
             hand_x[part, cols] = (
@@ -508,8 +507,8 @@
                 + zrh[part, cols].astype(F32)
             ).astype(BF16)
 
-        send(f"zl{h}", hand_x.at[part], zrl.at[part], p1)
-    query_slope(tiles * 3 // 4, tiles)
+        send(f"zl{k}", hand_x.at[part], zrl.at[part], p1)
+        query_slope(tiles * (12 + k) // 16, tiles * (13 + k) // 16)
     loss_finish(6)
     loss_ref[...] = lsum[...]
 
@@ -521,7 +520,8 @@
     outs = []
     for h in range(2):
         part = pl.ds(h * half, half)
-        arrived(f"zl{h}", zrl.at[part])
+        arrived(f"zl{2 * h}", zrl.at[parts[2 * h]])
+        arrived(f"zl{2 * h + 1}", zrl.at[parts[2 * h + 1]])
 
         @pl.loop(0, width // step)
         def _(t):

time: 214 us -> 173 us (0.81)
  Pallas kernels: 202 us -> 163 us
    pallas_call x1, Pallas kernels: 202 us -> 163 us  [shards(): pl.pallas_call(kernel, out_shape=(jax.ShapeDtypeStruct((8, 128), F32), ja...]
where the time goes in v2:
time: 173 us; the launch traced here: 172 us
  Pallas kernels  163 us (94%)
  local copies, waits for them, and re-layouts  6.95 us (4%)
  between operations  2.43 us (1%)
    pallas_call x1, Pallas kernels, shards(): pl.pallas_call(kernel, out_shape=(jax.ShapeDtypeStruct((8, 128), F32), ja...  163 us
    unnamed x4, local copies, waits for them, and re-layouts  5.76 us

profile of v2, /device:TPU:0, one launch (start us, length us, event | category | flops | bytes accessed | tf_op | source)
XLA Modules:
  0.0 172.4 jit_solution(4450200784730593861)
XLA Ops:
  0.6 163.1 %shard_map.67 = (f32[8,128]{1,0:T(8,128)}, bf16[512,4096]{1,0:T(8,128)(2,1)}, bf16[128,4096]{1,0:T(8,128)(2,1)}, bf16[1024,4096]{1,0:T(8,128)(2,1)}) custom-call(bf16[512,4096]{1,0:T(8,128)(2,1)} %q_hbm.1, bf16[128,4096]{1,0:T(8,128)(2,1)} %p_hbm.1, s32[1,512]{1,0:T(1,128)} %bitcast.3, s32[1,512]{1,0:T(1,128)} %bitcast.4), custom_call_target="tpu_custom_call" | custom-call | flops 38654705664 | bytes 41943040 | tf_op jit(solution)/shard_map/pallas_call | solution.py:556
  163.7 1.2 slice.3
  165.5 0.0 copy-start
  165.5 4.8 %copy.9 = bf16[512,4096]{1,0:T(8,128)(2,1)} copy(bf16[512,4096]{1,0:T(8,128)(2,1)} %get-tuple-element.13) | data formatting | bytes 8388608
  170.3 0.0 copy-done
  170.3 1.0 copy.10
Async XLA Ops:
  165.5 4.8 %copy-start = (bf16[128,4096]{1,0:T(8,128)(2,1)S(1)}, bf16[128,4096]{1,0:T(8,128)(2,1)}, u32[]{:S(2)}) copy-start(bf16[128,4096]{1,0:T(8,128)(2,1)} %get-tuple-element.14) | copy-start | bytes 3145732

commit v3 on v2

--- a/solution.py
+++ b/solution.py
@@ -11,7 +11,7 @@
 MESH = pl.DeviceIdType.MESH
 BF16 = jnp.bfloat16
 F32 = jnp.float32
-COPIES = 80
+COPIES = 112
 NT = (((1,), (1,)), ((), ()))
 
 
@@ -22,7 +22,7 @@
 def kernel(
     q_hbm, p_hbm, pos_ref, hid_ref,
     loss_ref, dq_hbm, dp_hbm, other_hbm,
-    lbuf, pbuf, qbuf, s, wt, wall, wht, xs, ys, xrf, xrs, yrf, yrs, zrh, zrl,
+    lbuf, pbuf, qbuf, s, wt, wall, wht, xs, ys, xrf, xrs, yrf, yrs, zrh, zrl, via, mix,
     ids, hs, hin, w2, top, lsum, lsend, lrecv, otile, dqt,
     ssem, rsem, csem,
 ):
@@ -72,24 +72,33 @@
         pl.semaphore_signal(barrier, inc=1, device_id=peer, device_id_type=MESH)
     pl.semaphore_wait(barrier, 7)
 
-    def lrow(xx, zz, h=0, n=p_dev):
-        return lbuf.at[rows((xx * 2 + zz) * p_dev + h * half, n)]
-
-    def prow(yy, zz, h=0, n=p_dev):
-        return pbuf.at[rows((yy * 2 + zz) * p_dev + h * half, n)]
+    quarter = half // 2
+    moved = half * 3 // 4
+    halves = [(0, half), (half, half)]
+    by_z = [(0, moved), (p_dev - moved, moved)]
+    direct = [(moved, half - moved), (half, half - moved)]
+    whole = (0, p_dev)
+
+    def lrow(xx, zz, part=whole):
+        return lbuf.at[rows((xx * 2 + zz) * p_dev + part[0], part[1], 16)]
+
+    def prow(yy, zz, part=whole):
+        return pbuf.at[rows((yy * 2 + zz) * p_dev + part[0], part[1], 16)]
 
     def orow(yy, zz):
         return other_hbm.at[rows((yy * 2 + zz) * p_dev, p_dev)]
 
     own = [p_hbm.at[pl.ds(h * half, half)] for h in range(2)]
-
+    quarters = [(k * quarter, quarter) for k in range(4)]
+
+    for k in range(4):
+        send(f"z{k}", p_hbm.at[pl.ds(k * quarter, quarter)], lrow(x, zl, quarters[k]), p1)
     for h in range(2):
-        send(f"z{h}", own[h], lrow(x, zl, h, half), p1)
-    for h in range(2):
-        send(f"x+o{h}", own[h], lrow(x, zl, h, half), xp)
-        send(f"x-o{1 - h}", own[1 - h], lrow(x, zl, 1 - h, half), xm)
-        send(f"y+o{h}", own[h], prow(y, zh, h, half), yp)
-        send(f"y-o{1 - h}", own[1 - h], prow(y, zh, 1 - h, half), ym)
+        r = 1 - h
+        send(f"x+o{h}", own[h], lrow(x, zl, halves[h]), xp)
+        send(f"x-o{r}", own[r], lrow(x, zl, halves[r]), xm)
+        send(f"y+o{h}", own[h], prow(y, zh, halves[h]), yp)
+        send(f"y-o{r}", own[r], prow(y, zh, halves[r]), ym)
     local = [
         pltpu.make_async_copy(q_hbm, qbuf.at[pl.ds(0, q_dev)], csem.at[0]),
         pltpu.make_async_copy(p_hbm, lrow(x, zl), csem.at[1]),
@@ -144,74 +153,98 @@
         copy.wait()
     score_loop(x, zl)
 
-    arrived("x+o0", lrow(px[3], zl, 0, half))
-    send("x+f", lrow(px[3], zl, 0, half), lrow(px[3], zl, 0, half), xp)
-    arrived("x-o1", lrow(px[1], zl, 1, half))
-    send("x-f", lrow(px[1], zl, 1, half), lrow(px[1], zl, 1, half), xm)
-    arrived("y+o0", prow(py[3], zh, 0, half))
-    send("y+f", prow(py[3], zh, 0, half), prow(py[3], zh, 0, half), yp)
-    arrived("y-o1", prow(py[1], zh, 1, half))
-    send("y-f", prow(py[1], zh, 1, half), prow(py[1], zh, 1, half), ym)
-    arrived("z0", lrow(x, oz, 0, half))
-    send("h0", lrow(x, oz, 0, half), prow(y, zh, 0, half), p2)
-    send("x+p0", lrow(x, oz, 0, half), lrow(x, oz, 0, half), xp)
+    def pass_x(name, xx, zz, part, peer):
+        send(name, lrow(xx, zz, part), lrow(xx, zz, part), peer)
+
+    def pass_y(name, yy, zz, part, peer):
+        send(name, prow(yy, zz, part), prow(yy, zz, part), peer)
+
+    def pass_z(k):
+        arrived(f"z{k}", lrow(x, oz, quarters[k]))
+        send(f"h{k}", lrow(x, oz, quarters[k]), prow(y, zh, quarters[k]), p2)
+
+    pass_z(0)
+    pass_z(1)
+    arrived("x+o0", lrow(px[3], zl, halves[0]))
+    pass_x("x+f", px[3], zl, halves[0], xp)
+    arrived("x-o1", lrow(px[1], zl, halves[1]))
+    pass_x("x-f", px[1], zl, halves[1], xm)
+    arrived("y+o0", prow(py[3], zh, halves[0]))
+    pass_y("y+f", py[3], zh, halves[0], yp)
+    arrived("y-o1", prow(py[1], zh, halves[1]))
+    pass_y("y-f", py[1], zh, halves[1], ym)
+    pass_x("x+p0", x, oz, halves[0], xp)
     arrived("ids", ids.at[1])
     arrived("q", qbuf.at[pl.ds(q_dev, q_dev)])
     score_pool(y, zh)
 
-    arrived("z1", lrow(x, oz, 1, half))
-    send("h1", lrow(x, oz, 1, half), prow(y, zh, 1, half), p2)
-    send("x-p1", lrow(x, oz, 1, half), lrow(x, oz, 1, half), xm)
-    send("x+p1", lrow(x, oz, 1, half), lrow(x, oz, 1, half), xp)
-    send("x-p0", lrow(x, oz, 0, half), lrow(x, oz, 0, half), xm)
-    arrived("h0", prow(y, oh, 0, half))
-    send("y+p0", prow(y, oh, 0, half), prow(y, oh, 0, half), yp)
+    pass_z(2)
+    arrived("h0", prow(y, oh, quarters[0]))
+    arrived("h1", prow(y, oh, quarters[1]))
+    pass_y("y+p0", y, oh, halves[0], yp)
+    pass_z(3)
+    pass_x("x-p1", x, oz, halves[1], xm)
+    pass_x("x+p1", x, oz, direct[1], xp)
+    pass_x("x-p0", x, oz, direct[0], xm)
+    arrived("x+o1", lrow(px[3], zl, halves[1]))
+    pass_x("zx1", px[3], zl, by_z[1], p1)
+    arrived("x-o0", lrow(px[1], zl, halves[0]))
+    pass_x("zx0", px[1], zl, by_z[0], p1)
+    arrived("y+o1", prow(py[3], zh, halves[1]))
+    send("ty1", prow(py[3], zh, by_z[1]), via.at[1], p2)
+    arrived("y-o0", prow(py[1], zh, halves[0]))
+    send("ty0", prow(py[1], zh, by_z[0]), via.at[0], p2)
+    send("o3", prow(py[3], zh), orow(py[3], zh), sib)
+    send("o1", prow(py[1], zh), orow(py[1], zh), sib)
     score_loop(x, oz)
-    arrived("x+o1", lrow(px[3], zl, 1, half))
     score_loop(px[3], zl)
-    arrived("x-o0", lrow(px[1], zl, 0, half))
     score_loop(px[1], zl)
-    arrived("y+o1", prow(py[3], zh, 1, half))
-    send("o3", prow(py[3], zh), orow(py[3], zh), sib)
+    arrived("h2", prow(y, oh, quarters[2]))
+    arrived("h3", prow(y, oh, quarters[3]))
+    pass_y("y-p1", y, oh, halves[1], ym)
+    pass_y("y+p1", y, oh, direct[1], yp)
+    pass_y("y-p0", y, oh, direct[0], ym)
+    send("op", prow(y, oh), orow(y, oh), sib)
     score_pool(py[3], zh)
-    arrived("y-o0", prow(py[1], zh, 0, half))
-    send("o1", prow(py[1], zh), orow(py[1], zh), sib)
-    arrived("h1", prow(y, oh, 1, half))
-    send("y-p1", prow(y, oh, 1, half), prow(y, oh, 1, half), ym)
-    send("y+p1", prow(y, oh, 1, half), prow(y, oh, 1, half), yp)
-    send("y-p0", prow(y, oh, 0, half), prow(y, oh, 0, half), ym)
-    send("op", prow(y, oh), orow(y, oh), sib)
     score_pool(py[1], zh)
-    arrived("x+f", lrow(px[2], zl, 0, half))
-    arrived("x-f", lrow(px[2], zl, 1, half))
+    arrived("x+f", lrow(px[2], zl, halves[0]))
+    arrived("x-f", lrow(px[2], zl, halves[1]))
     score_loop(px[2], zl)
-    arrived("y+f", prow(py[2], zh, 0, half))
-    arrived("y-f", prow(py[2], zh, 1, half))
+    arrived("ty1", via.at[1])
+    send("tz1", via.at[1], prow(py[3], oh, by_z[1]), p1)
+    score_pool(y, oh)
+    arrived("y+f", prow(py[2], zh, halves[0]))
+    arrived("y-f", prow(py[2], zh, halves[1]))
     send("o2", prow(py[2], zh), orow(py[2], zh), sib)
-    arrived("x+p0", lrow(px[3], oz, 0, half))
-    send("x+g", lrow(px[3], oz, 0, half), lrow(px[3], oz, 0, half), xp)
-    arrived("x-p1", lrow(px[1], oz, 1, half))
-    send("x-g", lrow(px[1], oz, 1, half), lrow(px[1], oz, 1, half), xm)
-    arrived("y+p0", prow(py[3], oh, 0, half))
-    send("y+g", prow(py[3], oh, 0, half), prow(py[3], oh, 0, half), yp)
-    arrived("y-p1", prow(py[1], oh, 1, half))
-    send("y-g", prow(py[1], oh, 1, half), prow(py[1], oh, 1, half), ym)
-    score_pool(y, oh)
     score_pool(py[2], zh)
-    arrived("x+p1", lrow(px[3], oz, 1, half))
+    arrived("x+p0", lrow(px[3], oz, halves[0]))
+    pass_x("x+g", px[3], oz, halves[0], xp)
+    arrived("x-p1", lrow(px[1], oz, halves[1]))
+    pass_x("x-g", px[1], oz, halves[1], xm)
+    arrived("y+p0", prow(py[3], oh, halves[0]))
+    pass_y("y+g", py[3], oh, halves[0], yp)
+    arrived("y-p1", prow(py[1], oh, halves[1]))
+    pass_y("y-g", py[1], oh, halves[1], ym)
+    arrived("ty0", via.at[0])
+    send("tz0", via.at[0], prow(py[1], oh, by_z[0]), p1)
+    arrived("x+p1", lrow(px[3], oz, direct[1]))
+    arrived("zx1", lrow(px[3], oz, by_z[1]))
     score_loop(px[3], oz)
-    arrived("x-p0", lrow(px[1], oz, 0, half))
+    arrived("x-p0", lrow(px[1], oz, direct[0]))
+    arrived("zx0", lrow(px[1], oz, by_z[0]))
     score_loop(px[1], oz)
-    arrived("y+p1", prow(py[3], oh, 1, half))
+    arrived("y+p1", prow(py[3], oh, direct[1]))
+    arrived("tz1", prow(py[3], oh, by_z[1]))
     score_pool(py[3], oh)
-    arrived("y-p0", prow(py[1], oh, 0, half))
+    arrived("y-p0", prow(py[1], oh, direct[0]))
+    arrived("tz0", prow(py[1], oh, by_z[0]))
     score_pool(py[1], oh)
-    arrived("y+g", prow(py[2], oh, 0, half))
-    arrived("y-g", prow(py[2], oh, 1, half))
+    arrived("y+g", prow(py[2], oh, halves[0]))
+    arrived("y-g", prow(py[2], oh, halves[1]))
     score_pool(py[2], oh)
     send("hs", hs.at[1], hin, sib)
-    arrived("x+g", lrow(px[2], oz, 0, half))
-    arrived("x-g", lrow(px[2], oz, 1, half))
+    arrived("x+g", lrow(px[2], oz, halves[0]))
+    arrived("x-g", lrow(px[2], oz, halves[1]))
     score_loop(px[2], oz)
 
     arrived("hs", hin)
@@ -304,40 +337,69 @@
     z_of = {"x": (oz, zl), "y": (oh, zh)}
     axes = {"x": (xs, xrf, xrs, xp, xm), "y": (ys, yrf, yrs, yp, ym)}
 
-    def piece(a, slot, role, h, n=half):
-        return axes[a][0].at[slot, rows(z_of[a][role] * p_dev + h * half, n)]
+    def piece(a, slot, role, part):
+        return axes[a][0].at[slot, rows(z_of[a][role] * p_dev + part[0], part[1], 16)]
+
+    def at(part):
+        return pl.ds(part[0], part[1])
+
+    def add_to(dst, *terms):
+        @pl.loop(0, width // step, unroll=2)
+        def _(t):
+            cols = rows(t * step, step, step)
+            total = dst[:, cols].astype(F32)
+            for term in terms:
+                total += term[:, cols].astype(F32)
+            dst[:, cols] = total.astype(BF16)
 
     def send_far(a, role):
         _, rf, _, plus, minus = axes[a]
-        send(f"{a}+s2{role}", piece(a, 2, role, 0), rf.at[0, role], plus)
-        send(f"{a}-s2{role}", piece(a, 2, role, 1), rf.at[1, role], minus)
+        send(f"{a}+s2{role}", piece(a, 2, role, halves[0]), rf.at[0, role], plus)
+        send(f"{a}-s2{role}", piece(a, 2, role, halves[1]), rf.at[1, role], minus)
 
     def send_near(a, role):
         _, _, rs, plus, minus = axes[a]
-        send(f"{a}+s1{role}", piece(a, 0, role, 1), rs.at[0, role, pl.ds(half, half)], plus)
-        send(f"{a}-s1{role}", piece(a, 1, role, 0), rs.at[1, role, pl.ds(0, half)], minus)
+        send(f"{a}+s1{role}", piece(a, 0, role, direct[1]), rs.at[0, role, at(direct[1])], plus)
+        send(f"{a}-s1{role}", piece(a, 1, role, direct[0]), rs.at[1, role, at(direct[0])], minus)
+
+    def send_mix_x():
+        send("mx1", piece("x", 0, 0, by_z[1]), mix.at[1], p1)
+        send("mx0", piece("x", 1, 0, by_z[0]), mix.at[0], p1)
+
+    hop = [xrs.at[1, 0, at(by_z[0])], xrs.at[0, 0, at(by_z[1])]]
+    end = [yrs.at[1, 0, at(by_z[0])], yrs.at[0, 0, at(by_z[1])]]
+
+    def send_mix_y():
+        send("my1", piece("y", 0, 0, by_z[1]), hop[1], p2)
+        send("my0", piece("y", 1, 0, by_z[0]), hop[0], p2)
+
+    def pass_mix_y(h):
+        arrived(f"my{h}", hop[h])
+        send(f"mz{h}", hop[h], end[h], p1)
+
+    def send_mixed(a, h):
+        _, _, rs, plus, minus = axes[a]
+        term = mix.at[h] if a == "x" else end[h]
+        arrived(f"mx{h}" if a == "x" else f"mz{h}", term)
+        mine = piece(a, 1 - h, 1, by_z[h])
+        add_to(mine, term)
+        send(f"{a}m{h}", mine, rs.at[1 - h, 1, at(by_z[h])], plus if h else minus)
 
     def send_sum(a, role):
         _, rf, rs, plus, minus = axes[a]
-        for d, (sign, slot, h, peer) in enumerate((("+", 0, 0, plus), ("-", 1, 1, minus))):
+        for d, (sign, peer) in enumerate((("+", plus), ("-", minus))):
             arrived(f"{a}{sign}s2{role}", rf.at[d, role])
-            mine = piece(a, slot, role, h)
-
-            @pl.loop(0, width // step)
-            def _(t):
-                cols = rows(t * step, step, step)
-                mine[:, cols] = (
-                    mine[:, cols].astype(F32) + rf[d, role, :, cols].astype(F32)
-                ).astype(BF16)
-
-            send(f"{a}{sign}s0{role}", mine, rs.at[d, role, pl.ds(h * half, half)], peer)
+            mine = piece(a, d, role, halves[d])
+            add_to(mine, rf.at[d, role])
+            send(f"{a}{sign}s0{role}", mine, rs.at[d, role, at(halves[d])], peer)
 
     def sums_arrived(a, role):
         rs = axes[a][2]
         for d, sign in enumerate("+-"):
-            near = 1 - d
-            arrived(f"{a}{sign}s1{role}", rs.at[d, role, pl.ds(near * half, half)])
-            arrived(f"{a}{sign}s0{role}", rs.at[d, role, pl.ds(d * half, half)])
+            arrived(f"{a}{sign}s1{role}", rs.at[d, role, at(direct[1 - d])])
+            if role:
+                arrived(f"{a}m{1 - d}", rs.at[d, role, at(by_z[1 - d])])
+            arrived(f"{a}{sign}s0{role}", rs.at[d, role, at(halves[d])])
 
     x_part(2)
     send_far("x", 0)
@@ -354,11 +416,13 @@
     x_part(1)
     x_part(3)
     send_near("x", 0)
+    send_mix_x()
     loss_finish(2)
     loss_start(3)
     y_part(1)
     y_part(3)
     send_near("y", 0)
+    send_mix_y()
     loss_finish(3)
     loss_start(4)
     send_sum("x", 0)
@@ -395,6 +459,9 @@
     pool_weights(y, 0, 0)
     pool_weights(y, 1, p_dev)
     pool_part(2 * p_dev, store_y)
+    pass_mix_y(1)
+    send_mixed("x", 1)
+    send_mixed("x", 0)
 
     for c in range(blocks):
         wall[:, c * p_dev:(c + 1) * p_dev] = (
@@ -472,43 +539,29 @@
             dqt[k] = (scale * acc).astype(BF16)
             tile_out(t).start()
 
-    query_slope(0, tiles * 3 // 4)
+    query_slope(0, tiles // 4)
+    pass_mix_y(0)
     loss_finish(5)
     loss_start(6)
-
-    quarter = half // 2
-    parts = [pl.ds(k * quarter, quarter) for k in range(4)]
+    query_slope(tiles // 4, tiles * 3 // 8)
+
+    parts = [pl.ds(0, moved), pl.ds(moved, p_dev - 2 * moved), pl.ds(p_dev - moved, moved)]
+    signs = [(0,), (0, 1), (1,)]
     sums_arrived("y", 0)
     for k, part in enumerate(parts):
-
-        @pl.loop(0, width // step, unroll=2)
-        def _(t):
-            cols = rows(t * step, step, step)
-            hand_y[part, cols] = (
-                hand_y[part, cols].astype(F32)
-                + yrs[0, 0, part, cols].astype(F32)
-                + yrs[1, 0, part, cols].astype(F32)
-            ).astype(BF16)
-
+        add_to(hand_y.at[part], *(yrs.at[d, 0, part] for d in signs[k]))
         send(f"zh{k}", hand_y.at[part], zrh.at[part], p2)
+    send_mixed("y", 1)
+    query_slope(tiles * 3 // 8, tiles * 5 // 8)
     sums_arrived("x", 0)
+    send_mixed("y", 0)
     send_sum("x", 1)
     send_sum("y", 1)
     for k, part in enumerate(parts):
         arrived(f"zh{k}", zrh.at[part])
-
-        @pl.loop(0, width // step, unroll=2)
-        def _(t):
-            cols = rows(t * step, step, step)
-            hand_x[part, cols] = (
-                hand_x[part, cols].astype(F32)
-                + xrs[0, 0, part, cols].astype(F32)
-                + xrs[1, 0, part, cols].astype(F32)
-                + zrh[part, cols].astype(F32)
-            ).astype(BF16)
-
+        add_to(hand_x.at[part], zrh.at[part], *(xrs.at[d, 0, part] for d in signs[k]))
         send(f"zl{k}", hand_x.at[part], zrl.at[part], p1)
-        query_slope(tiles * (12 + k) // 16, tiles * (13 + k) // 16)
+        query_slope(tiles * (10 + 2 * k) // 16, tiles * (12 + 2 * k) // 16)
     loss_finish(6)
     loss_ref[...] = lsum[...]
 
@@ -518,12 +571,10 @@
     sent("y-s21")
     result = ys.at[2, rows(zh * p_dev, p_dev)]
     outs = []
-    for h in range(2):
-        part = pl.ds(h * half, half)
-        arrived(f"zl{2 * h}", zrl.at[parts[2 * h]])
-        arrived(f"zl{2 * h + 1}", zrl.at[parts[2 * h + 1]])
-
-        @pl.loop(0, width // step)
+    for h, part in enumerate(parts):
+        arrived(f"zl{h}", zrl.at[part])
+
+        @pl.loop(0, width // step, unroll=2)
         def _(t):
             cols = rows(t * step, step, step)
             result[part, cols] = (
@@ -535,7 +586,7 @@
                 + zrl[part, cols].astype(F32)
             ).astype(BF16)
 
-        copy = pltpu.make_async_copy(result.at[part], dp_hbm.at[part], csem.at[h])
+        copy = pltpu.make_async_copy(result.at[part], dp_hbm.at[part], csem.at[4 + h])
         copy.start()
         outs.append(copy)
     tile_out(tiles - 2).wait()
@@ -550,6 +601,7 @@
     q_dev, width = queries.shape
     p_dev = passages.shape[0]
     half = p_dev // 2
+    moved = half * 3 // 4
     vmem = pltpu.VMEM
     hbm = pl.BlockSpec(memory_space=pl.ANY)
     block = pl.BlockSpec(memory_space=pltpu.VMEM)
@@ -579,6 +631,8 @@
             vmem((2, 2, p_dev, width), BF16),
             vmem((p_dev, width), BF16),
             vmem((p_dev, width), BF16),
+            vmem((2, moved, width), BF16),
+            vmem((2, moved, width), BF16),
             vmem((2, 8, q_dev), jnp.int32),
             vmem((2, 8, q_dev), F32),
             vmem((8, q_dev), F32),
@@ -591,7 +645,7 @@
             vmem((2, q_dev, 256), BF16),
             pltpu.SemaphoreType.DMA((COPIES,)),
             pltpu.SemaphoreType.DMA((COPIES,)),
-            pltpu.SemaphoreType.DMA((4,)),
+            pltpu.SemaphoreType.DMA((7,)),
         ],
         compiler_params=pltpu.CompilerParams(
             collective_id=0, has_side_effects=True, vmem_limit_bytes=63 * 2**20

time: 173 us -> 156 us (0.902)
  Pallas kernels: 163 us -> 146 us
    pallas_call x1, Pallas kernels: 163 us -> 146 us  [shards(): pl.pallas_call(kernel, out_shape=(jax.ShapeDtypeStruct((8, 128), F32), ja...]
where the time goes in v3:
time: 156 us
  Pallas kernels  146 us (94%)
  local copies, waits for them, and re-layouts  6.95 us (4%)
  between operations  2.43 us (2%)
    pallas_call x1, Pallas kernels, shards(): pl.pallas_call(kernel, out_shape=(jax.ShapeDtypeStruct((8, 128), F32), ja...  146 us
    unnamed x4, local copies, waits for them, and re-layouts  5.76 us

profile of v3, /device:TPU:0, one launch (start us, length us, event | category | flops | bytes accessed | tf_op | source)
XLA Modules:
  0.0 155.5 jit_solution(15297688278176411269)
XLA Ops:
  0.6 146.2 %shard_map.67 = (f32[8,128]{1,0:T(8,128)}, bf16[512,4096]{1,0:T(8,128)(2,1)}, bf16[128,4096]{1,0:T(8,128)(2,1)}, bf16[1024,4096]{1,0:T(8,128)(2,1)}) custom-call(bf16[512,4096]{1,0:T(8,128)(2,1)} %q_hbm.1, bf16[128,4096]{1,0:T(8,128)(2,1)} %p_hbm.1, s32[1,512]{1,0:T(1,128)} %bitcast.3, s32[1,512]{1,0:T(1,128)} %bitcast.4), custom_call_target="tpu_custom_call" | custom-call | flops 38654705664 | bytes 41943040 | tf_op jit(solution)/shard_map/pallas_call | solution.py:608
  146.8 1.2 slice.3
  148.6 0.0 copy-start
  148.7 4.8 %copy.9 = bf16[512,4096]{1,0:T(8,128)(2,1)} copy(bf16[512,4096]{1,0:T(8,128)(2,1)} %get-tuple-element.13) | data formatting | bytes 8388608
  153.4 0.0 copy-done
  153.4 1.0 copy.10
Async XLA Ops:
  148.6 4.8 %copy-start = (bf16[128,4096]{1,0:T(8,128)(2,1)S(1)}, bf16[128,4096]{1,0:T(8,128)(2,1)}, u32[]{:S(2)}) copy-start(bf16[128,4096]{1,0:T(8,128)(2,1)} %get-tuple-element.14) | copy-start | bytes 3145732
